TPU v7x, 32 devices: a whole 2x2x4 slice. The times are simulated.
32 devices in a mesh: band: 16 (over z, y, x), group: 2 (over core).
Axes of the slice: x: 2, y: 2, z: 4, core: 2. Of those that a mesh axis runs over, the one named last changes fastest.
Arguments:
- trial: bfloat16 [16, 64, 4096], P('band'), may hold values from -6 to 6
- orbitals: bfloat16 [32, 64, 4096], P(('band', 'group')), may hold values from -6 to 6
- labels: int32 [32], P(('band', 'group')), may hold values from 0 to 31, each once
- kernel_mask: int32 [64, 4096], replicated, may hold values from 0 to 1, as said below
Outputs:
- exchange_field: float32 [16, 64, 4096], P('band', 'group')
Inputs may be any that keep to these rules, and one draw needn't show every extreme that they name: `labels`: a permutation of the source orbitals' numbers. `kernel_mask`: unchanged when any one frequency index k is replaced by (64 - k) mod 64.
All inputs are finite; a program needn't handle non-finite values.
Results may differ from a plain program's by a relative error of at most 0.009.
Values may be sent and summed in bfloat16 or wider, within the bound.
A program may use at most 64 MiB of HBM per device.

v0:
```python
import jax
import jax.numpy as jnp
from jax import lax
from jax.sharding import PartitionSpec as P

WINDOW = 2


screen_square = 16.0


def passed_along(value, axis, steps):
    count = lax.axis_size(axis)
    pairs = [(source, (source + steps) % count) for source in range(count)]
    return lax.ppermute(value, axis, pairs)


def cas_table(grid_size):
    frequency = jnp.arange(grid_size, dtype=jnp.int32)
    product = frequency[:, None] * frequency[None, :] % grid_size
    phase_angle = product.astype(jnp.float32) * (2.0 * jnp.pi / grid_size)
    return (
        (jnp.cos(phase_angle) + jnp.sin(phase_angle)) / jnp.sqrt(jnp.float32(grid_size))
    ).astype(jnp.bfloat16)


def screened_kernel(mask_cube):
    grid_size = mask_cube.shape[0]
    frequency = jnp.arange(grid_size, dtype=jnp.int32)
    signed = jnp.where(frequency < grid_size // 2, frequency, frequency - grid_size)
    squared = signed * signed
    q_square = squared[:, None, None] + squared[None, :, None] + squared[None, None, :]
    return (
        mask_cube.astype(jnp.float32)
        * screen_square
        / (q_square.astype(jnp.float32) + screen_square)
    )


def occupation(label_values, orbital_count):
    shifted = (label_values.astype(jnp.float32) - orbital_count / 2.0) / (orbital_count / 4.0)
    return 1.0 / (1.0 + jnp.exp(shifted))


def axis_pass(field_data, hartley):
    return lax.dot_general(
        field_data, hartley, (((0,), (0,)), ((), ())), preferred_element_type=jnp.float32
    )


def pair_contribution(target, source_orbital, weight, hartley, kernel):
    density = (target.astype(jnp.float32) * source_orbital.astype(jnp.float32)).astype(jnp.bfloat16)
    first = axis_pass(density, hartley).astype(jnp.bfloat16)
    second = axis_pass(first, hartley).astype(jnp.bfloat16)
    spectrum = (axis_pass(second, hartley) * kernel).astype(jnp.bfloat16)
    back_first = axis_pass(spectrum, hartley).astype(jnp.bfloat16)
    back_second = axis_pass(back_first, hartley).astype(jnp.bfloat16)
    potential = axis_pass(back_second, hartley)
    return weight * potential * source_orbital.astype(jnp.float32)


def shards(trial, orbitals, labels, kernel_mask):
    grid_size = trial.shape[1]
    orbital_count = lax.axis_size("band") * lax.axis_size("group")
    hartley = cas_table(grid_size)
    kernel = screened_kernel(kernel_mask.reshape(grid_size, grid_size, grid_size))
    target = trial[0].reshape(grid_size, grid_size, grid_size)
    sources = []
    current, current_tags = (orbitals, labels)
    for offset in range(WINDOW):
        sources.append((current[0], current_tags[0]))
        if offset + 1 < WINDOW:
            current, current_tags = passed_along((current, current_tags), "band", -1)
    field_total = None
    for source_orbital, source_label in sources:
        weight = occupation(source_label, orbital_count)
        contribution = pair_contribution(
            target, source_orbital.reshape(grid_size, grid_size, grid_size), weight, hartley, kernel
        )
        contribution = contribution.reshape(1, grid_size, grid_size * grid_size)
        field_total = contribution if field_total is None else field_total + contribution
    field_total = lax.psum_scatter(
        field_total.astype(jnp.bfloat16), "group", scatter_dimension=1, tiled=True
    ).astype(jnp.float32)
    return -field_total


def solution(mesh):
    in_specs = (P("band", None, None), P(("band", "group"), None, None), P(("band", "group")), P())
    out_specs = P("band", "group", None)
    return jax.shard_map(shards, mesh=mesh, in_specs=in_specs, out_specs=out_specs, check_vma=False)
```

profile of v0, /device:TPU:31, one launch (start us, length us, event | category | flops | bytes accessed | tf_op | source)
XLA Modules:
  0.0 80.5 jit_solution(403627424332771239)
XLA Ops:
  6.5 0.3 collective-permute-start.1
  6.8 1.2 %collective-permute-start = (s32[1]{0:T(128)}, s32[1]{0:T(128)}, u32[]{:S(2)}, u32[]{:S(2)}) collective-permute-start(s32[1]{0:T(128)} %param.6), channel_id=1, source_target_pairs={{0,30},{2,0},{4,2},{6,4},{8,6},{10,8},{12,10},{14,12},{16,14},{18,... | collective-permute-start | bytes 20 | tf_op jit(solution)/shard_map/ppermute | solution.py:15
  7.9 1.3 %convert_multiply_fusion = f32[64,4096]{1,0:T(8,128)S(1)} fusion(s32[64,4096]{1,0:T(8,128)} %param.7), kind=kLoop, calls=%fused_computation.23 | loop fusion | flops 524288 | bytes 2097152 | tf_op jit(solution)/shard_map/mul | solution.py:34
  9.3 1.9 %reshape.112 = f32[64,64,64]{2,1,0:T(8,128)S(1)} reshape(bf16[1,64,4096]{2,1,0:T(8,128)(2,1)} %param.5) | data formatting | bytes 1572864 | tf_op jit(solution)/shard_map/convert_element_type | solution.py:52
  11.9 3.0 %reshape.111 = f32[64,64,64]{2,1,0:T(8,128)} reshape(bf16[1,64,4096]{2,1,0:T(8,128)(2,1)} %param.4) | data formatting | bytes 1572864 | tf_op jit(solution)/shard_map/convert_element_type | solution.py:52
  14.9 2.1 %mul.166 = f32[64,64,64]{2,1,0:T(8,128)} reshape(f32[64,4096]{1,0:T(8,128)S(1)} %convert_multiply_fusion) | data formatting | bytes 2097152 | tf_op jit(solution)/shard_map/mul | solution.py:34
  17.2 6.1 %collective-permute-done = s32[1]{0:T(128)} collective-permute-done((s32[1]{0:T(128)}, s32[1]{0:T(128)}, u32[]{:S(2)}, u32[]{:S(2)}) %collective-permute-start) | collective-permute-done | bytes 36 | tf_op jit(solution)/shard_map/ppermute | solution.py:15
  24.0 3.0 %reshape.115 = f32[64,64,64]{2,1,0:T(8,128)} reshape(bf16[1,64,4096]{2,1,0:T(8,128)(2,1)} %collective-permute-done.1) | data formatting | bytes 1572864 | tf_op jit(solution)/shard_map/convert_element_type | solution.py:52
  27.0 4.0 %multiply_convert_fusion.1 = (bf16[64,64,64]{2,1,0:T(8,128)(2,1)}, bf16[64,64,64]{2,1,0:T(8,128)(2,1)S(1)}) fusion(f32[64,64,64]{2,1,0:T(8,128)} %reshape.111, f32[64,64,64]{2,1,0:T(8,128)} %reshape.115, f32[64,64,64]{2,1,0:T(8,128)S(1)} %reshape.112), kind=kLoop, calls=%fused_computation.2 | loop fusion | flops 1048576 | bytes 4194304 | tf_op jit(solution)/shard_map/convert_element_type | solution.py:52
  31.0 1.1 %convolution_convert_fusion.7 = bf16[64,64,64]{2,1,0:T(8,128)(2,1)S(1)} fusion(bf16[64,64,64]{2,1,0:T(8,128)(2,1)S(1)} %get-tuple-element.6), kind=kOutput, calls=%fused_computation.13 | convolution fusion | flops 33886208 | bytes 1048576 | tf_op jit(solution)/shard_map/dot_general | solution.py:46
  32.1 1.1 %convolution_convert_fusion.6 = bf16[64,64,64]{2,1,0:T(8,128)(2,1)S(1)} fusion(bf16[64,64,64]{2,1,0:T(8,128)(2,1)S(1)} %convolution_convert_fusion.7), kind=kOutput, calls=%fused_computation.12 | convolution fusion | flops 33886208 | bytes 1048576 | tf_op jit(solution)/shard_map/dot_general | solution.py:46
  33.2 1.5 %multiply_convert_fusion.2 = bf16[64,64,64]{2,1,0:T(8,128)(2,1)S(1)} fusion(bf16[64,64,64]{2,1,0:T(8,128)(2,1)S(1)} %convolution_convert_fusion.6, f32[64,64,64]{2,1,0:T(8,128)S(1)} %copy-done, s32[64]{0:T(128)S(1)} %fusion.64, s32[64,64]{1,0:T(8,128)S(1)} %broadcast_add_fusion), kind=kOutput, calls=%fused_computation.3 | convolution fusion | flops 35196928 | bytes 2113792 | tf_op jit(solution)/shard_map/dot_general | solution.py:46
  34.7 2.1 %convolution_convert_fusion.5 = bf16[64,64,64]{2,1,0:T(8,128)(2,1)} fusion(bf16[64,64,64]{2,1,0:T(8,128)(2,1)S(1)} %multiply_convert_fusion.2), kind=kOutput, calls=%fused_computation.11 | convolution fusion | flops 33886208 | bytes 1048576 | tf_op jit(solution)/shard_map/dot_general | solution.py:46
  36.8 3.5 %copy.9 = bf16[64,64,64]{0,1,2:T(8,128)(2,1)S(1)} copy(bf16[64,64,64]{2,1,0:T(8,128)(2,1)} %convolution_convert_fusion.5) | data formatting | bytes 1048576 | tf_op jit(solution)/shard_map/convert_element_type | solution.py:56
  40.3 2.9 %fusion = f32[64,64,64]{2,1,0:T(8,128)} fusion(bf16[64,64,64]{0,1,2:T(8,128)(2,1)S(1)} %copy.9), kind=kOutput, calls=%fused_computation.14 | convolution fusion | flops 67510272 | bytes 1572864 | tf_op jit(solution)/shard_map/dot_general | solution.py:46
  43.1 2.4 %convolution_convert_fusion.3 = bf16[64,64,64]{2,1,0:T(8,128)(2,1)S(1)} fusion(bf16[64,64,64]{2,1,0:T(8,128)(2,1)} %get-tuple-element.5), kind=kOutput, calls=%fused_computation.9 | convolution fusion | flops 33886208 | bytes 1048576 | tf_op jit(solution)/shard_map/dot_general | solution.py:46
  45.6 1.1 %convolution_convert_fusion.2 = bf16[64,64,64]{2,1,0:T(8,128)(2,1)S(1)} fusion(bf16[64,64,64]{2,1,0:T(8,128)(2,1)S(1)} %convolution_convert_fusion.3), kind=kOutput, calls=%fused_computation.8 | convolution fusion | flops 33886208 | bytes 1048576 | tf_op jit(solution)/shard_map/dot_general | solution.py:46
  46.7 1.5 %multiply_convert_fusion = bf16[64,64,64]{2,1,0:T(8,128)(2,1)S(1)} fusion(bf16[64,64,64]{2,1,0:T(8,128)(2,1)S(1)} %convolution_convert_fusion.2, f32[64,64,64]{2,1,0:T(8,128)S(1)} %copy-done.1, s32[64]{0:T(128)S(1)} %fusion.64, s32[64,64]{1,0:T(8,128)S(1)} %broadcast_add_fusion), kind=kOutput, calls=%fused_computation.1 | convolution fusion | flops 35196928 | bytes 2113792 | tf_op jit(solution)/shard_map/dot_general | solution.py:46
  48.2 2.1 %convolution_convert_fusion.1 = bf16[64,64,64]{2,1,0:T(8,128)(2,1)} fusion(bf16[64,64,64]{2,1,0:T(8,128)(2,1)S(1)} %multiply_convert_fusion), kind=kOutput, calls=%fused_computation.7 | convolution fusion | flops 33886208 | bytes 1048576 | tf_op jit(solution)/shard_map/dot_general | solution.py:46
  50.3 3.3 %copy.14 = bf16[64,64,64]{0,1,2:T(8,128)(2,1)S(1)} copy(bf16[64,64,64]{2,1,0:T(8,128)(2,1)} %convolution_convert_fusion.1) | data formatting | bytes 1048576 | tf_op jit(solution)/shard_map/convert_element_type | solution.py:56
  53.6 4.9 %add_convert_fusion = bf16[64,64,64]{2,1,0:T(8,128)(2,1)} fusion(f32[64,64,64]{2,1,0:T(8,128)} %reshape.115, f32[64,64,64]{2,1,0:T(8,128)S(1)} %reshape.112, f32[64,64,64]{2,1,0:T(8,128)} %fusion, bf16[64,64,64]{0,1,2:T(8,128)(2,1)S(1)} %copy.14, f32[]{:T(128)} %bitcast.2, f32[]{:T(128)} %bitcast), kind=kOutput, calls=%fused_computation | convolution fusion | flops 69083136 | bytes 4194312 | tf_op jit(solution)/shard_map/dot_general | solution.py:46
  58.5 2.7 %convert_element_type.164 = bf16[1,64,4096]{2,1,0:T(8,128)(2,1)} reshape(bf16[64,64,64]{2,1,0:T(8,128)(2,1)} %add_convert_fusion) | data formatting | bytes 1048576 | tf_op jit(solution)/shard_map/convert_element_type | solution.py:83
  61.2 10.6 %reduce-scatter.2.cloned.1.call-done = bf16[1,32,4096]{2,1,0:T(8,128)(2,1)} async-done(((bf16[1,64,4096]{2,1,0:T(8,128)(2,1)}), bf16[1,32,4096]{2,1,0:T(8,128)(2,1)}) %reduce-scatter.2.cloned.1.call-update) | async-done | bytes 262160 | tf_op jit(solution)/shard_map/reduce_scatter | solution.py:82
  71.9 1.8 %convert_negate_fusion = f32[1,32,4096]{2,1,0:T(8,128)} fusion(bf16[1,32,4096]{2,1,0:T(8,128)(2,1)} %reduce-scatter.2.cloned.1.call-done), kind=kLoop, calls=%fused_computation.24 | loop fusion | flops 262144 | bytes 786432 | tf_op jit(solution)/shard_map/neg | solution.py:85
  (9 shorter events, 0.1 us)
Async XLA Ops:
  6.5 65.3 %reduce-scatter.2.cloned.1.call-start = ((), (), s32[]{:S(2)}) async-start(), calls=%async_computation.1 | async-start | bytes 786432 | tf_op jit(solution)/shard_map/reduce_scatter | solution.py:82
  6.5 17.5 %collective-permute-start.1 = (bf16[1,64,4096]{2,1,0:T(8,128)(2,1)}, bf16[1,64,4096]{2,1,0:T(8,128)(2,1)}, u32[]{:S(2)}, u32[]{:S(2)}) collective-permute-start(bf16[1,64,4096]{2,1,0:T(8,128)(2,1)} %param.5), channel_id=1, source_target_pairs={{0,30},{2,0},{4,2},{6,4},{8,6},{10,8},{12,10},{14,12},{16,14},{18,... | collective-permute-start | bytes 1572872 | tf_op jit(solution)/shard_map/ppermute | solution.py:15
  6.8 16.4 %collective-permute-start = (s32[1]{0:T(128)}, s32[1]{0:T(128)}, u32[]{:S(2)}, u32[]{:S(2)}) collective-permute-start(s32[1]{0:T(128)} %param.6), channel_id=1, source_target_pairs={{0,30},{2,0},{4,2},{6,4},{8,6},{10,8},{12,10},{14,12},{16,14},{18,... | collective-permute-start | bytes 20 | tf_op jit(solution)/shard_map/ppermute | solution.py:15
  31.0 2.1 %copy-start = (f32[64,64,64]{2,1,0:T(8,128)S(1)}, f32[64,64,64]{2,1,0:T(8,128)}, u32[]{:S(2)}) copy-start(f32[64,64,64]{2,1,0:T(8,128)} %mul.166) | copy-start | bytes 3145732
  43.1 3.5 %copy-start.1 = (f32[64,64,64]{2,1,0:T(8,128)S(1)}, f32[64,64,64]{2,1,0:T(8,128)}, u32[]{:S(2)}) copy-start(f32[64,64,64]{2,1,0:T(8,128)} %mul.166) | copy-start | bytes 3145732
Sparse Core Ops, SparseCore 0:
  61.4 10.4 reduce-scatter.1
where the time goes:
time: 81.9 us; the launch traced here: 80.5 us
  matrix products  20.6 us (25%)
  local copies, waits for them, and re-layouts  19.6 us (24%)
  waiting for transfers between devices  16.7 us (20%)
  between operations  15 us (18%)
  other arithmetic  7.16 us (9%)
  starting transfers between devices  1.41 us (2%)
    dot_general x10, matrix products, axis_pass(): lax.dot_general(field_data, hartley, (((0,), (0,)), ((), ())), preferred_...  20.6 us
    reduce_scatter x1, waiting for transfers between devices, shards(): lax.psum_scatter(field_total.astype(jnp.bfloat16), 'group', scatter_dimen...  10.6 us
    convert_element_type x2, local copies, waits for them, and re-layouts, pair_contribution(): back_first = axis_pass(spectrum, hartley).astype(jnp.bfloat16)  6.78 us
    ppermute x2, waiting for transfers between devices, passed_along(): return lax.ppermute(value, axis, pairs)  6.07 us
    convert_element_type x2, local copies, waits for them, and re-layouts, pair_contribution(): source_orbital.astype(jnp.float32)  4.97 us
    convert_element_type x1, other arithmetic, pair_contribution(): (target.astype(jnp.float32) * source_orbital.astype(jnp.float32)).astype(...  4 us
    convert_element_type x1, local copies, waits for them, and re-layouts, pair_contribution(): target.astype(jnp.float32) * source_orbital.astype(jnp.float32)  3.01 us
    convert_element_type x1, local copies, waits for them, and re-layouts, shards(): field_total.astype(jnp.bfloat16)  2.71 us
  transfers between devices with their start and end apart: 3, of which 2 were waited for; matrix products, arithmetic and copies ran while one was open for 11% of the time, Pallas kernels for 0%

commit v1 on v0

v1 whole, which is shorter than its diff:
```python
import functools

import jax
import jax.numpy as jnp
import ml_dtypes
import numpy as np
from jax import lax
from jax.experimental import pallas as pl
from jax.experimental.pallas import tpu as pltpu
from jax.sharding import PartitionSpec as P

screen_square = 16.0

STACK = 4
PAD = 8


def cas_blocks(grid_size):
    frequency = np.arange(grid_size)
    angle = (np.outer(frequency, frequency) % grid_size) * (2.0 * np.pi / grid_size)
    table = (np.cos(angle) + np.sin(angle)) / np.sqrt(grid_size)
    blocks = np.kron(np.eye(STACK), table).astype(np.float32)
    return jnp.asarray(blocks.astype(ml_dtypes.bfloat16))


def occupation(label_values, orbital_count):
    shifted = (label_values.astype(jnp.float32) - orbital_count / 2.0) / (orbital_count / 4.0)
    return 1.0 / (1.0 + jnp.exp(shifted))


def signed_square(index, grid_size):
    signed = jnp.where(index < grid_size // 2, index, index - grid_size)
    return (signed * signed).astype(jnp.float32)


def exchange_kernel(
    n, bands, groups,
    trial_hbm, orbital_hbm, label_ref, mask_hbm, blocks_ref, out_ref,
    target, own, other, mask, cube, coulomb, field, label_own, label_other,
    give, take, local_sem, send_sem, recv_sem, label_send, label_recv, give_sem, take_sem,
):
    band, group = lax.axis_index("band"), lax.axis_index("group")
    before = lax.rem(band + bands - 1, bands)
    after = lax.rem(band + 1, bands)
    half, lanes, wide = n // 2, 2 * n, STACK * n
    chunk = STACK * wide
    chunks = n * n // chunk
    planes = chunk // n
    pitch = n + PAD
    rows = n // groups
    mesh_id = pl.DeviceIdType.MESH

    def columns(c):
        return pl.ds(c * chunk, chunk)

    local = [
        pltpu.make_async_copy(orbital_hbm.at[0], own, local_sem.at[0]),
        pltpu.make_async_copy(trial_hbm.at[0], target, local_sem.at[1]),
        pltpu.make_async_copy(mask_hbm, mask, local_sem.at[2]),
    ]
    for copy in local:
        copy.start()
    label_own[...] = jnp.full(label_own.shape, label_ref[0], jnp.int32)

    barrier = pltpu.get_barrier_semaphore()
    peers = [lax.rem(group + k, groups) for k in range(1, groups)]
    for neighbour in (before, after):
        pl.semaphore_signal(barrier, inc=1, device_id={"band": neighbour}, device_id_type=mesh_id)
    for peer in peers:
        pl.semaphore_signal(barrier, inc=1, device_id={"group": peer}, device_id_type=mesh_id)
    pl.semaphore_wait(barrier, 2 + len(peers))

    sent = []
    for c in range(chunks):
        sent.append(pltpu.make_async_remote_copy(
            src_ref=orbital_hbm.at[0, :, columns(c)], dst_ref=other.at[:, columns(c)],
            send_sem=send_sem.at[c], recv_sem=recv_sem.at[c],
            device_id={"band": before}, device_id_type=mesh_id))
        sent[-1].start()
    label_copy = pltpu.make_async_remote_copy(
        src_ref=label_own, dst_ref=label_other, send_sem=label_send, recv_sem=label_recv,
        device_id={"band": before}, device_id_type=mesh_id)
    label_copy.start()

    blocks = blocks_ref[...]
    left = lax.broadcasted_iota(jnp.int32, (half, lanes), 1) < n

    def matmul(a, b):
        return jnp.dot(a, b, preferred_element_type=jnp.float32)

    def exchanged(value):
        low, high = value[:half], value[half:]
        first = jnp.where(left, low, pltpu.roll(high, n, 1))
        second = jnp.where(left, pltpu.roll(low, n, 1), high)
        return first, second

    def restored(first, second):
        low = jnp.where(left, first, pltpu.roll(second, n, 1))
        high = jnp.where(left, pltpu.roll(first, n, 1), second)
        return jnp.concatenate([low, high], axis=0)

    def put_planes(ref, plane, value):
        for step, part in enumerate(exchanged(value)):
            ref[pl.ds(plane + step, half, stride=pitch), :] = part

    def forward(c, source):
        pieces = []
        for q in range(STACK):
            place = pl.ds(c * chunk + q * wide, wide)
            density = target[:, place].astype(jnp.float32) * source[:, place].astype(jnp.float32)
            pieces.append(density.astype(jnp.bfloat16))
        first = matmul(blocks, jnp.concatenate(pieces, axis=0)).astype(jnp.bfloat16)
        second = matmul(first, blocks)
        for q in range(STACK):
            for h in range(wide // lanes):
                put_planes(cube, c * planes + q * STACK + 2 * h,
                           second[q * n:(q + 1) * n, h * lanes:(h + 1) * lanes])

    def middle():
        for start in range(0, half, 2 * STACK):
            def gathered(ref):
                return jnp.concatenate([
                    jnp.concatenate([
                        ref[pl.ds((start + side * STACK + q) * pitch, n), :] for q in range(STACK)
                    ], axis=0) for side in range(2)
                ], axis=1)
            spectrum = matmul(blocks, gathered(cube).astype(jnp.bfloat16)) * gathered(coulomb)
            back = matmul(blocks, spectrum.astype(jnp.bfloat16))
            for side in range(2):
                for q in range(STACK):
                    cube[pl.ds((start + side * STACK + q) * pitch, n), :] = (
                        back[q * n:(q + 1) * n, side * lanes:(side + 1) * lanes])

    def backward(c, source, weight, accumulate):
        pieces = []
        for q in range(STACK):
            pairs = []
            for h in range(wide // lanes):
                plane = c * planes + q * STACK + 2 * h
                pairs.append(restored(cube[pl.ds(plane, half, stride=pitch), :],
                                      cube[pl.ds(plane + 1, half, stride=pitch), :]))
            pieces.append(jnp.concatenate(pairs, axis=1).astype(jnp.bfloat16))
        back = matmul(blocks, jnp.concatenate(pieces, axis=0)).astype(jnp.bfloat16)
        potential = matmul(back, blocks)
        for q in range(STACK):
            place = pl.ds(c * chunk + q * wide, wide)
            part = weight * potential[q * n:(q + 1) * n] * source[:, place].astype(jnp.float32)
            field[:, place] = field[:, place] + part if accumulate else part

    local[2].wait()
    ky_lane = lax.broadcasted_iota(jnp.int32, (n, lanes), 1)
    kx_row = lax.broadcasted_iota(jnp.int32, (n, lanes), 0)
    base = signed_square(kx_row, n) + signed_square(lax.rem(ky_lane, n), n) + screen_square
    for t in range(n // 2):
        ky = 2 * t + jnp.where(ky_lane < n, 0, 1)
        kept = mask[:, pl.ds(t * lanes, lanes)].astype(jnp.float32)
        put_planes(coulomb, 2 * t, kept * (screen_square / (base + signed_square(ky, n))))

    local[0].wait()
    local[1].wait()
    orbital_count = bands * groups
    for c in range(chunks):
        forward(c, own)
    middle()
    weight = occupation(label_own[0:1, :], orbital_count)
    for c in range(chunks):
        backward(c, own, weight, False)

    for c in range(chunks):
        sent[c].wait_recv()
        forward(c, other)
    middle()
    label_copy.wait_recv()
    weight = occupation(label_other[0:1, :], orbital_count)
    passed = []
    for c in range(chunks):
        backward(c, other, weight, True)
        for k, peer in enumerate(peers):
            give[k, :, columns(c)] = field[pl.ds(pl.multiple_of(peer * rows, rows), rows), columns(c)].astype(jnp.bfloat16)
            copy = pltpu.make_async_remote_copy(
                src_ref=give.at[k, :, columns(c)], dst_ref=take.at[k, :, columns(c)],
                send_sem=give_sem.at[k, c], recv_sem=take_sem.at[k, c],
                device_id={"group": peer}, device_id_type=mesh_id)
            copy.start()
            passed.append((c, k, copy))
    for c in range(chunks):
        total = field[pl.ds(pl.multiple_of(group * rows, rows), rows), columns(c)]
        for at, k, copy in passed:
            if at == c:
                copy.wait_recv()
                total = total + take[k, :, columns(c)].astype(jnp.float32)
        out_ref[0, :, columns(c)] = -total
    for _, _, copy in passed:
        copy.wait_send()
    for copy in sent:
        copy.wait_send()
    label_copy.wait_send()


def shards(trial, orbitals, labels, kernel_mask):
    n = trial.shape[1]
    bands, groups = lax.axis_size("band"), lax.axis_size("group")
    rows = n // groups
    chunks = n // (STACK * STACK)
    peers = groups - 1
    vmem = pl.BlockSpec(memory_space=pltpu.VMEM)
    anywhere = pl.BlockSpec(memory_space=pl.ANY)
    dma = pltpu.SemaphoreType.DMA
    return pl.pallas_call(
        functools.partial(exchange_kernel, n, bands, groups),
        out_shape=jax.ShapeDtypeStruct((1, rows, n * n), jnp.float32),
        in_specs=[anywhere, anywhere, pl.BlockSpec(memory_space=pltpu.SMEM), anywhere, vmem],
        out_specs=vmem,
        scratch_shapes=[
            pltpu.VMEM((n, n * n), jnp.bfloat16),
            pltpu.VMEM((n, n * n), jnp.bfloat16),
            pltpu.VMEM((n, n * n), jnp.bfloat16),
            pltpu.VMEM((n, n * n), jnp.int32),
            pltpu.VMEM((n // 2 * (n + PAD), 2 * n), jnp.float32),
            pltpu.VMEM((n // 2 * (n + PAD), 2 * n), jnp.float32),
            pltpu.VMEM((n, n * n), jnp.float32),
            pltpu.VMEM((8, STACK * n), jnp.int32),
            pltpu.VMEM((8, STACK * n), jnp.int32),
            pltpu.VMEM((peers, rows, n * n), jnp.bfloat16),
            pltpu.VMEM((peers, rows, n * n), jnp.bfloat16),
            dma((3,)), dma((chunks,)), dma((chunks,)), dma, dma, dma((peers, chunks)), dma((peers, chunks)),
        ],
        compiler_params=pltpu.CompilerParams(
            collective_id=0, has_side_effects=True, vmem_limit_bytes=40 * 1024 * 1024),
        name="exchange",
    )(trial, orbitals, labels, kernel_mask, cas_blocks(n))


def solution(mesh):
    in_specs = (P("band", None, None), P(("band", "group"), None, None), P(("band", "group")), P())
    out_specs = P("band", "group", None)
    return jax.shard_map(shards, mesh=mesh, in_specs=in_specs, out_specs=out_specs, check_vma=False)
```

time: 81.9 us -> 27.8 us (0.34); the launches traced: 80.5 us -> 27.6 us
  Pallas kernels: 0 us -> 21.9 us
  matrix products: 20.6 us -> 0 us
  waiting for transfers between devices: 16.7 us -> 0 us
  local copies, waits for them, and re-layouts: 19.6 us -> 5 us
  between operations: 15 us -> 0.67 us
  other arithmetic: 7.16 us -> 0 us
  starting transfers between devices: 1.41 us -> 0 us
    pallas_call x0 -> x1, Pallas kernels: none -> 21.9 us  [shards(): pl.pallas_call(functools.partial(exchange_kernel, n, bands, groups), out_...]
    dot_general x10 -> x0, matrix products: 20.6 us -> none  [axis_pass(): lax.dot_general(field_data, hartley, (((0,), (0,)), ((), ())), preferred_...]
    convert_element_type x6 -> x0, local copies, waits for them, and re-layouts: 17.5 us -> none  [the longest x2 6.78 us: pair_contribution(): back_first = axis_pass(spectrum, hartley).astype(jnp.bfloat16)]
    reduce_scatter x1 -> x0, waiting for transfers between devices: 10.6 us -> none  [shards(): lax.psum_scatter(field_total.astype(jnp.bfloat16), 'group', scatter_dimen...]
    ppermute x2 -> x0, waiting for transfers between devices: 6.07 us -> none  [passed_along(): return lax.ppermute(value, axis, pairs)]
    unnamed x4 -> x9, local copies, waits for them, and re-layouts: 0.01 us -> 5 us
    convert_element_type x1 -> x0, other arithmetic: 4 us -> none  [pair_contribution(): (target.astype(jnp.float32) * source_orbital.astype(jnp.float32)).astype(...]
    mul x1 -> x0, local copies, waits for them, and re-layouts: 2.14 us -> none  [screened_kernel(): mask_cube.astype(jnp.float32) * screen_square]
  transfers between devices with their start and end apart: 3 -> 0, of which waited for: 2 -> 0; matrix products, arithmetic and copies ran while one was open for 11% -> 0% of each run, Pallas kernels for 0% -> 0%
where the time goes in v1:
time: 27.8 us; the launch traced here: 27.6 us
  Pallas kernels  21.9 us (79%)
  local copies, waits for them, and re-layouts  5 us (18%)
  between operations  0.67 us (2%)
    pallas_call x1, Pallas kernels, shards(): pl.pallas_call(functools.partial(exchange_kernel, n, bands, groups), out_...  21.9 us
    unnamed x9, local copies, waits for them, and re-layouts  5 us

profile of v1, /device:TPU:31, one launch (start us, length us, event | category | flops | bytes accessed | tf_op | source)
XLA Modules:
  0.0 27.6 jit_solution(5398492865555465343)
XLA Ops:
  0.7 0.0 copy-start
  0.7 1.2 %copy-done = s32[64,4096]{1,0:T(8,128)S(1)} copy-done((s32[64,4096]{1,0:T(8,128)S(1)}, s32[64,4096]{1,0:T(8,128)}, u32[]{:S(2)}) %copy-start) | copy-done | bytes 1048600
  1.9 0.0 copy-start.1
  1.9 1.0 %copy-done.1 = bf16[1,64,4096]{2,1,0:T(8,128)(2,1)S(1)} copy-done((bf16[1,64,4096]{2,1,0:T(8,128)(2,1)S(1)}, bf16[1,64,4096]{2,1,0:T(8,128)(2,1)}, u32[]{:S(2)}) %copy-start.1) | copy-done | bytes 524312
  2.9 0.0 copy-start.2
  2.9 1.0 %copy-done.2 = bf16[1,64,4096]{2,1,0:T(8,128)(2,1)S(1)} copy-done((bf16[1,64,4096]{2,1,0:T(8,128)(2,1)S(1)}, bf16[1,64,4096]{2,1,0:T(8,128)(2,1)}, u32[]{:S(2)}) %copy-start.2) | copy-done | bytes 524312
  4.0 0.0 copy-start.3
  4.0 0.9 %copy-done.3 = bf16[256,256]{1,0:T(8,128)(2,1)S(1)} copy-done((bf16[256,256]{1,0:T(8,128)(2,1)S(1)}, bf16[256,256]{1,0:T(8,128)(2,1)}, u32[]{:S(2)}) %copy-start.3) | copy-done | bytes 131096
  4.9 21.9 %exchange.1 = f32[1,32,4096]{2,1,0:T(8,128)S(1)} custom-call(bf16[1,64,4096]{2,1,0:T(8,128)(2,1)S(1)} %copy-done.1, bf16[1,64,4096]{2,1,0:T(8,128)(2,1)S(1)} %copy-done.2, s32[1]{0:T(128)S(6)} %copy.7.label_ref, s32[64,4096]{1,0:T(8,128)S(1)} %copy-done, bf16[256,256]{1,0:T(8,128)(2,1)S(1)} %copy-done.3), custom_call_target="tpu_custom_call" | custom-call | tf_op jit(solution)/shard_map/exchange/pallas_call | solution.py:209
  26.8 0.8 %copy.8 = f32[1,32,4096]{2,1,0:T(8,128)} copy(f32[1,32,4096]{2,1,0:T(8,128)S(1)} %exchange.1) | data formatting | bytes 1048576
Async XLA Ops:
  0.7 1.2 %copy-start = (s32[64,4096]{1,0:T(8,128)S(1)}, s32[64,4096]{1,0:T(8,128)}, u32[]{:S(2)}) copy-start(s32[64,4096]{1,0:T(8,128)} %mask_hbm.1) | copy-start | bytes 3145732
  1.9 1.0 %copy-start.1 = (bf16[1,64,4096]{2,1,0:T(8,128)(2,1)S(1)}, bf16[1,64,4096]{2,1,0:T(8,128)(2,1)}, u32[]{:S(2)}) copy-start(bf16[1,64,4096]{2,1,0:T(8,128)(2,1)} %trial_hbm.1) | copy-start | bytes 1572868
  2.9 1.0 %copy-start.2 = (bf16[1,64,4096]{2,1,0:T(8,128)(2,1)S(1)}, bf16[1,64,4096]{2,1,0:T(8,128)(2,1)}, u32[]{:S(2)}) copy-start(bf16[1,64,4096]{2,1,0:T(8,128)(2,1)} %orbital_hbm.1) | copy-start | bytes 1572868
  4.0 0.9 %copy-start.3 = (bf16[256,256]{1,0:T(8,128)(2,1)S(1)}, bf16[256,256]{1,0:T(8,128)(2,1)}, u32[]{:S(2)}) copy-start(bf16[256,256]{1,0:T(8,128)(2,1)} %constant.2.clone.blocks_ref) | copy-start | bytes 393220

commit v2 on v1

--- a/solution.py
+++ b/solution.py
@@ -35,8 +35,8 @@
 
 def exchange_kernel(
     n, bands, groups,
-    trial_hbm, orbital_hbm, label_ref, mask_hbm, blocks_ref, out_ref,
-    target, own, other, mask, cube, coulomb, field, label_own, label_other,
+    trial_hbm, orbital_hbm, label_ref, mask_hbm, blocks_hbm, out_ref,
+    table, target, own, other, mask, cube, coulomb, field, label_own, label_other,
     give, take, local_sem, send_sem, recv_sem, label_send, label_recv, give_sem, take_sem,
 ):
     band, group = lax.axis_index("band"), lax.axis_index("group")
@@ -57,9 +57,8 @@
         pltpu.make_async_copy(orbital_hbm.at[0], own, local_sem.at[0]),
         pltpu.make_async_copy(trial_hbm.at[0], target, local_sem.at[1]),
         pltpu.make_async_copy(mask_hbm, mask, local_sem.at[2]),
+        pltpu.make_async_copy(blocks_hbm, table, local_sem.at[3]),
     ]
-    for copy in local:
-        copy.start()
     label_own[...] = jnp.full(label_own.shape, label_ref[0], jnp.int32)
 
     barrier = pltpu.get_barrier_semaphore()
@@ -81,8 +80,9 @@
         src_ref=label_own, dst_ref=label_other, send_sem=label_send, recv_sem=label_recv,
         device_id={"band": before}, device_id_type=mesh_id)
     label_copy.start()
-
-    blocks = blocks_ref[...]
+    for at in (2, 0, 1, 3):
+        local[at].start()
+
     left = lax.broadcasted_iota(jnp.int32, (half, lanes), 1) < n
 
     def matmul(a, b):
@@ -107,8 +107,7 @@
         pieces = []
         for q in range(STACK):
             place = pl.ds(c * chunk + q * wide, wide)
-            density = target[:, place].astype(jnp.float32) * source[:, place].astype(jnp.float32)
-            pieces.append(density.astype(jnp.bfloat16))
+            pieces.append(target[:, place] * source[:, place])
         first = matmul(blocks, jnp.concatenate(pieces, axis=0)).astype(jnp.bfloat16)
         second = matmul(first, blocks)
         for q in range(STACK):
@@ -158,6 +157,8 @@
 
     local[0].wait()
     local[1].wait()
+    local[3].wait()
+    blocks = table[...]
     orbital_count = bands * groups
     for c in range(chunks):
         forward(c, own)
@@ -204,14 +205,15 @@
     chunks = n // (STACK * STACK)
     peers = groups - 1
     vmem = pl.BlockSpec(memory_space=pltpu.VMEM)
-    anywhere = pl.BlockSpec(memory_space=pl.ANY)
+    hbm = pl.BlockSpec(memory_space=pltpu.HBM)
     dma = pltpu.SemaphoreType.DMA
     return pl.pallas_call(
         functools.partial(exchange_kernel, n, bands, groups),
         out_shape=jax.ShapeDtypeStruct((1, rows, n * n), jnp.float32),
-        in_specs=[anywhere, anywhere, pl.BlockSpec(memory_space=pltpu.SMEM), anywhere, vmem],
+        in_specs=[hbm, hbm, pl.BlockSpec(memory_space=pltpu.SMEM), hbm, hbm],
         out_specs=vmem,
         scratch_shapes=[
+            pltpu.VMEM((STACK * n, STACK * n), jnp.bfloat16),
             pltpu.VMEM((n, n * n), jnp.bfloat16),
             pltpu.VMEM((n, n * n), jnp.bfloat16),
             pltpu.VMEM((n, n * n), jnp.bfloat16),
@@ -223,10 +225,10 @@
             pltpu.VMEM((8, STACK * n), jnp.int32),
             pltpu.VMEM((peers, rows, n * n), jnp.bfloat16),
             pltpu.VMEM((peers, rows, n * n), jnp.bfloat16),
-            dma((3,)), dma((chunks,)), dma((chunks,)), dma, dma, dma((peers, chunks)), dma((peers, chunks)),
+            dma((4,)), dma((chunks,)), dma((chunks,)), dma, dma, dma((peers, chunks)), dma((peers, chunks)),
         ],
         compiler_params=pltpu.CompilerParams(
-            collective_id=0, has_side_effects=True, vmem_limit_bytes=40 * 1024 * 1024),
+            collective_id=0, has_side_effects=True, vmem_limit_bytes=63 * 1024 * 1024),
         name="exchange",
     )(trial, orbitals, labels, kernel_mask, cas_blocks(n))
 

time: 27.8 us -> 25.5 us (0.917)
  local copies, waits for them, and re-layouts: 5 us -> 1.87 us
  Pallas kernels: 21.9 us -> 22.8 us
    unnamed x9 -> x1, local copies, waits for them, and re-layouts: 5 us -> 1.87 us
    pallas_call x1, Pallas kernels: 21.9 us -> 22.8 us  [shards(): pl.pallas_call(functools.partial(exchange_kernel, n, bands, groups), out_...]
where the time goes in v2:
time: 25.5 us; the launch traced here: 25.3 us
  Pallas kernels  22.8 us (89%)
  local copies, waits for them, and re-layouts  1.87 us (7%)
  between operations  0.66 us (3%)
    pallas_call x1, Pallas kernels, shards(): pl.pallas_call(functools.partial(exchange_kernel, n, bands, groups), out_...  22.8 us
    unnamed x1, local copies, waits for them, and re-layouts  1.87 us

profile of v2, /device:TPU:31, one launch (start us, length us, event | category | flops | bytes accessed | tf_op | source)
XLA Modules:
  0.0 25.3 jit_solution(2548821447815370985)
XLA Ops:
  0.7 22.8 %exchange.1 = f32[1,32,4096]{2,1,0:T(8,128)} custom-call(bf16[1,64,4096]{2,1,0:T(8,128)(2,1)} %trial_hbm.1, bf16[1,64,4096]{2,1,0:T(8,128)(2,1)} %orbital_hbm.1, s32[1]{0:T(128)S(6)} %copy.7.label_ref, s32[64,4096]{1,0:T(8,128)} %mask_hbm.1, bf16[256,256]{1,0:T(8,128)(2,1)} %constant.2.clone.blocks_hbm), custom_call_target="tpu_custom_call" | custom-call | tf_op jit(solution)/shard_map/exchange/pallas_call | solution.py:210
  23.4 1.9 %copy.8 = f32[1,32,4096]{2,1,0:T(8,128)} copy(f32[1,32,4096]{2,1,0:T(8,128)} %exchange.1) | data formatting | bytes 1048576

commit v3 on v2

--- a/solution.py
+++ b/solution.py
@@ -12,7 +12,7 @@
 screen_square = 16.0
 
 STACK = 4
-PAD = 8
+PAD = 1
 
 
 def cas_blocks(grid_size):
@@ -36,7 +36,7 @@
 def exchange_kernel(
     n, bands, groups,
     trial_hbm, orbital_hbm, label_ref, mask_hbm, blocks_hbm, out_ref,
-    table, target, own, other, mask, cube, coulomb, field, label_own, label_other,
+    table, target, own, other, mask, cube, filtered, coulomb, field, label_own, label_other,
     give, take, local_sem, send_sem, recv_sem, label_send, label_recv, give_sem, take_sem,
 ):
     band, group = lax.axis_index("band"), lax.axis_index("group")
@@ -127,7 +127,7 @@
             back = matmul(blocks, spectrum.astype(jnp.bfloat16))
             for side in range(2):
                 for q in range(STACK):
-                    cube[pl.ds((start + side * STACK + q) * pitch, n), :] = (
+                    filtered[pl.ds((start + side * STACK + q) * pitch, n), :] = (
                         back[q * n:(q + 1) * n, side * lanes:(side + 1) * lanes])
 
     def backward(c, source, weight, accumulate):
@@ -136,8 +136,8 @@
             pairs = []
             for h in range(wide // lanes):
                 plane = c * planes + q * STACK + 2 * h
-                pairs.append(restored(cube[pl.ds(plane, half, stride=pitch), :],
-                                      cube[pl.ds(plane + 1, half, stride=pitch), :]))
+                pairs.append(restored(filtered[pl.ds(plane, half, stride=pitch), :],
+                                      filtered[pl.ds(plane + 1, half, stride=pitch), :]))
             pieces.append(jnp.concatenate(pairs, axis=1).astype(jnp.bfloat16))
         back = matmul(blocks, jnp.concatenate(pieces, axis=0)).astype(jnp.bfloat16)
         potential = matmul(back, blocks)
@@ -220,6 +220,7 @@
             pltpu.VMEM((n, n * n), jnp.int32),
             pltpu.VMEM((n // 2 * (n + PAD), 2 * n), jnp.float32),
             pltpu.VMEM((n // 2 * (n + PAD), 2 * n), jnp.float32),
+            pltpu.VMEM((n // 2 * (n + PAD), 2 * n), jnp.float32),
             pltpu.VMEM((n, n * n), jnp.float32),
             pltpu.VMEM((8, STACK * n), jnp.int32),
             pltpu.VMEM((8, STACK * n), jnp.int32),

time: 25.5 us -> 25.5 us (level)
  no operation moved by 1% of the time
where the time goes in v3:
time: 25.5 us; the launch traced here: 25.3 us
  Pallas kernels  22.8 us (89%)
  local copies, waits for them, and re-layouts  1.87 us (7%)
  between operations  0.66 us (3%)
    pallas_call x1, Pallas kernels, shards(): pl.pallas_call(functools.partial(exchange_kernel, n, bands, groups), out_...  22.8 us
    unnamed x1, local copies, waits for them, and re-layouts  1.87 us

profile of v3, /device:TPU:31, one launch (start us, length us, event | category | flops | bytes accessed | tf_op | source)
XLA Modules:
  0.0 25.3 jit_solution(455081996343008351)
XLA Ops:
  0.7 22.8 %exchange.1 = f32[1,32,4096]{2,1,0:T(8,128)} custom-call(bf16[1,64,4096]{2,1,0:T(8,128)(2,1)} %trial_hbm.1, bf16[1,64,4096]{2,1,0:T(8,128)(2,1)} %orbital_hbm.1, s32[1]{0:T(128)S(6)} %copy.7.label_ref, s32[64,4096]{1,0:T(8,128)} %mask_hbm.1, bf16[256,256]{1,0:T(8,128)(2,1)} %constant.2.clone.blocks_hbm), custom_call_target="tpu_custom_call" | custom-call | tf_op jit(solution)/shard_map/exchange/pallas_call | solution.py:210
  23.4 1.9 %copy.8 = f32[1,32,4096]{2,1,0:T(8,128)} copy(f32[1,32,4096]{2,1,0:T(8,128)} %exchange.1) | data formatting | bytes 1048576

commit v4 on v3

--- a/solution.py
+++ b/solution.py
@@ -36,7 +36,7 @@
 def exchange_kernel(
     n, bands, groups,
     trial_hbm, orbital_hbm, label_ref, mask_hbm, blocks_hbm, out_ref,
-    table, target, own, other, mask, cube, filtered, coulomb, field, label_own, label_other,
+    table, target, own, other, mask, staged, back, cube, filtered, coulomb, field, label_own, label_other,
     give, take, local_sem, send_sem, recv_sem, label_send, label_recv, give_sem, take_sem,
 ):
     band, group = lax.axis_index("band"), lax.axis_index("group")
@@ -103,44 +103,53 @@
         for step, part in enumerate(exchanged(value)):
             ref[pl.ds(plane + step, half, stride=pitch), :] = part
 
-    def forward(c, source):
-        pieces = []
-        for q in range(STACK):
-            place = pl.ds(c * chunk + q * wide, wide)
-            pieces.append(target[:, place] * source[:, place])
-        first = matmul(blocks, jnp.concatenate(pieces, axis=0)).astype(jnp.bfloat16)
-        second = matmul(first, blocks)
-        for q in range(STACK):
+    def forward(group_of_chunks, source):
+        for c in group_of_chunks:
+            pieces = []
+            for q in range(STACK):
+                place = pl.ds(c * chunk + q * wide, wide)
+                pieces.append(target[:, place] * source[:, place])
+            staged[pl.ds(c * wide, wide), :] = matmul(
+                blocks, jnp.concatenate(pieces, axis=0)).astype(jnp.bfloat16)
+        begin, count = group_of_chunks[0], len(group_of_chunks)
+        second = matmul(staged[pl.ds(begin * wide, count * wide), :], blocks)
+        for q in range(count * STACK):
             for h in range(wide // lanes):
-                put_planes(cube, c * planes + q * STACK + 2 * h,
+                put_planes(cube, begin * planes + q * STACK + 2 * h,
                            second[q * n:(q + 1) * n, h * lanes:(h + 1) * lanes])
 
     def middle():
-        for start in range(0, half, 2 * STACK):
-            def gathered(ref):
-                return jnp.concatenate([
-                    jnp.concatenate([
-                        ref[pl.ds((start + side * STACK + q) * pitch, n), :] for q in range(STACK)
-                    ], axis=0) for side in range(2)
-                ], axis=1)
-            spectrum = matmul(blocks, gathered(cube).astype(jnp.bfloat16)) * gathered(coulomb)
-            back = matmul(blocks, spectrum.astype(jnp.bfloat16))
+        starts = range(0, half, 2 * STACK)
+
+        def gathered(ref, start):
+            return jnp.concatenate([
+                jnp.concatenate([
+                    ref[pl.ds((start + side * STACK + q) * pitch, n), :] for q in range(STACK)
+                ], axis=0) for side in range(2)
+            ], axis=1)
+
+        for step, start in enumerate(starts):
+            spectrum = matmul(blocks, gathered(cube, start).astype(jnp.bfloat16)) * gathered(coulomb, start)
+            staged[pl.ds(step * wide, wide), :] = spectrum.astype(jnp.bfloat16)
+        for step, start in enumerate(starts):
+            result = matmul(blocks, staged[pl.ds(step * wide, wide), :])
             for side in range(2):
                 for q in range(STACK):
                     filtered[pl.ds((start + side * STACK + q) * pitch, n), :] = (
-                        back[q * n:(q + 1) * n, side * lanes:(side + 1) * lanes])
-
-    def backward(c, source, weight, accumulate):
-        pieces = []
-        for q in range(STACK):
-            pairs = []
-            for h in range(wide // lanes):
-                plane = c * planes + q * STACK + 2 * h
-                pairs.append(restored(filtered[pl.ds(plane, half, stride=pitch), :],
-                                      filtered[pl.ds(plane + 1, half, stride=pitch), :]))
-            pieces.append(jnp.concatenate(pairs, axis=1).astype(jnp.bfloat16))
-        back = matmul(blocks, jnp.concatenate(pieces, axis=0)).astype(jnp.bfloat16)
-        potential = matmul(back, blocks)
+                        result[q * n:(q + 1) * n, side * lanes:(side + 1) * lanes])
+
+    def backward_z():
+        for c in range(chunks):
+            for q in range(STACK):
+                for h in range(wide // lanes):
+                    plane = c * planes + q * STACK + 2 * h
+                    pair = restored(filtered[pl.ds(plane, half, stride=pitch), :],
+                                    filtered[pl.ds(plane + 1, half, stride=pitch), :])
+                    staged[pl.ds(c * wide + q * n, n), pl.ds(h * lanes, lanes)] = pair.astype(jnp.bfloat16)
+        back[...] = matmul(staged[...], blocks).astype(jnp.bfloat16)
+
+    def backward_x(c, source, weight, accumulate):
+        potential = matmul(blocks, back[pl.ds(c * wide, wide), :])
         for q in range(STACK):
             place = pl.ds(c * chunk + q * wide, wide)
             part = weight * potential[q * n:(q + 1) * n] * source[:, place].astype(jnp.float32)
@@ -160,22 +169,23 @@
     local[3].wait()
     blocks = table[...]
     orbital_count = bands * groups
-    for c in range(chunks):
-        forward(c, own)
+    forward(range(chunks), own)
     middle()
+    backward_z()
     weight = occupation(label_own[0:1, :], orbital_count)
     for c in range(chunks):
-        backward(c, own, weight, False)
+        backward_x(c, own, weight, False)
 
     for c in range(chunks):
         sent[c].wait_recv()
-        forward(c, other)
+        forward([c], other)
     middle()
+    backward_z()
     label_copy.wait_recv()
     weight = occupation(label_other[0:1, :], orbital_count)
     passed = []
     for c in range(chunks):
-        backward(c, other, weight, True)
+        backward_x(c, other, weight, True)
         for k, peer in enumerate(peers):
             give[k, :, columns(c)] = field[pl.ds(pl.multiple_of(peer * rows, rows), rows), columns(c)].astype(jnp.bfloat16)
             copy = pltpu.make_async_remote_copy(
@@ -218,6 +228,8 @@
             pltpu.VMEM((n, n * n), jnp.bfloat16),
             pltpu.VMEM((n, n * n), jnp.bfloat16),
             pltpu.VMEM((n, n * n), jnp.int32),
+            pltpu.VMEM((n * n // STACK, STACK * n), jnp.bfloat16),
+            pltpu.VMEM((n * n // STACK, STACK * n), jnp.bfloat16),
             pltpu.VMEM((n // 2 * (n + PAD), 2 * n), jnp.float32),
             pltpu.VMEM((n // 2 * (n + PAD), 2 * n), jnp.float32),
             pltpu.VMEM((n // 2 * (n + PAD), 2 * n), jnp.float32),

time: 25.5 us -> 24.7 us (0.969)
  Pallas kernels: 22.8 us -> 22 us
    pallas_call x1, Pallas kernels: 22.8 us -> 22 us  [shards(): pl.pallas_call(functools.partial(exchange_kernel, n, bands, groups), out_...]
where the time goes in v4:
time: 24.7 us; the launch traced here: 24.5 us
  Pallas kernels  22 us (89%)
  local copies, waits for them, and re-layouts  1.87 us (8%)
  between operations  0.66 us (3%)
    pallas_call x1, Pallas kernels, shards(): pl.pallas_call(functools.partial(exchange_kernel, n, bands, groups), out_...  22 us
    unnamed x1, local copies, waits for them, and re-layouts  1.87 us

profile of v4, /device:TPU:31, one launch (start us, length us, event | category | flops | bytes accessed | tf_op | source)
XLA Modules:
  0.0 24.5 jit_solution(8462840498866440335)
XLA Ops:
  0.7 22.0 %exchange.1 = f32[1,32,4096]{2,1,0:T(8,128)} custom-call(bf16[1,64,4096]{2,1,0:T(8,128)(2,1)} %trial_hbm.1, bf16[1,64,4096]{2,1,0:T(8,128)(2,1)} %orbital_hbm.1, s32[1]{0:T(128)S(6)} %copy.7.label_ref, s32[64,4096]{1,0:T(8,128)} %mask_hbm.1, bf16[256,256]{1,0:T(8,128)(2,1)} %constant.2.clone.blocks_hbm), custom_call_target="tpu_custom_call" | custom-call | tf_op jit(solution)/shard_map/exchange/pallas_call | solution.py:220
  22.6 1.9 %copy.8 = f32[1,32,4096]{2,1,0:T(8,128)} copy(f32[1,32,4096]{2,1,0:T(8,128)} %exchange.1) | data formatting | bytes 1048576

commit v5 on v4

--- a/solution.py
+++ b/solution.py
@@ -35,9 +35,9 @@
 
 def exchange_kernel(
     n, bands, groups,
-    trial_hbm, orbital_hbm, label_ref, mask_hbm, blocks_hbm, out_ref,
-    table, target, own, other, mask, staged, back, cube, filtered, coulomb, field, label_own, label_other,
-    give, take, local_sem, send_sem, recv_sem, label_send, label_recv, give_sem, take_sem,
+    trial_hbm, orbital_hbm, label_ref, mask_hbm, blocks_hbm, out_hbm,
+    table, result_part, target, own, other, mask, staged, back, cube, filtered, coulomb, field, label_own, label_other,
+    give, take, local_sem, send_sem, recv_sem, label_send, label_recv, give_sem, take_sem, out_sem,
 ):
     band, group = lax.axis_index("band"), lax.axis_index("group")
     before = lax.rem(band + bands - 1, bands)
@@ -59,6 +59,8 @@
         pltpu.make_async_copy(mask_hbm, mask, local_sem.at[2]),
         pltpu.make_async_copy(blocks_hbm, table, local_sem.at[3]),
     ]
+    for at in (2, 0, 1, 3):
+        local[at].start()
     label_own[...] = jnp.full(label_own.shape, label_ref[0], jnp.int32)
 
     barrier = pltpu.get_barrier_semaphore()
@@ -80,8 +82,6 @@
         src_ref=label_own, dst_ref=label_other, send_sem=label_send, recv_sem=label_recv,
         device_id={"band": before}, device_id_type=mesh_id)
     label_copy.start()
-    for at in (2, 0, 1, 3):
-        local[at].start()
 
     left = lax.broadcasted_iota(jnp.int32, (half, lanes), 1) < n
 
@@ -104,13 +104,16 @@
             ref[pl.ds(plane + step, half, stride=pitch), :] = part
 
     def forward(group_of_chunks, source):
+        density = []
         for c in group_of_chunks:
             pieces = []
             for q in range(STACK):
                 place = pl.ds(c * chunk + q * wide, wide)
                 pieces.append(target[:, place] * source[:, place])
-            staged[pl.ds(c * wide, wide), :] = matmul(
-                blocks, jnp.concatenate(pieces, axis=0)).astype(jnp.bfloat16)
+            density.append(jnp.concatenate(pieces, axis=0))
+        first = matmul(blocks, jnp.concatenate(density, axis=1)).astype(jnp.bfloat16)
+        for step, c in enumerate(group_of_chunks):
+            staged[pl.ds(c * wide, wide), :] = first[:, step * wide:(step + 1) * wide]
         begin, count = group_of_chunks[0], len(group_of_chunks)
         second = matmul(staged[pl.ds(begin * wide, count * wide), :], blocks)
         for q in range(count * STACK):
@@ -119,24 +122,21 @@
                            second[q * n:(q + 1) * n, h * lanes:(h + 1) * lanes])
 
     def middle():
-        starts = range(0, half, 2 * STACK)
-
-        def gathered(ref, start):
+        sides = range(half // STACK)
+
+        def gathered(ref):
             return jnp.concatenate([
                 jnp.concatenate([
-                    ref[pl.ds((start + side * STACK + q) * pitch, n), :] for q in range(STACK)
-                ], axis=0) for side in range(2)
+                    ref[pl.ds((side * STACK + q) * pitch, n), :] for q in range(STACK)
+                ], axis=0) for side in sides
             ], axis=1)
 
-        for step, start in enumerate(starts):
-            spectrum = matmul(blocks, gathered(cube, start).astype(jnp.bfloat16)) * gathered(coulomb, start)
-            staged[pl.ds(step * wide, wide), :] = spectrum.astype(jnp.bfloat16)
-        for step, start in enumerate(starts):
-            result = matmul(blocks, staged[pl.ds(step * wide, wide), :])
-            for side in range(2):
-                for q in range(STACK):
-                    filtered[pl.ds((start + side * STACK + q) * pitch, n), :] = (
-                        result[q * n:(q + 1) * n, side * lanes:(side + 1) * lanes])
+        spectrum = matmul(blocks, gathered(cube).astype(jnp.bfloat16)) * gathered(coulomb)
+        result = matmul(blocks, spectrum.astype(jnp.bfloat16))
+        for side in sides:
+            for q in range(STACK):
+                filtered[pl.ds((side * STACK + q) * pitch, n), :] = (
+                    result[q * n:(q + 1) * n, side * lanes:(side + 1) * lanes])
 
     def backward_z():
         for c in range(chunks):
@@ -148,12 +148,15 @@
                     staged[pl.ds(c * wide + q * n, n), pl.ds(h * lanes, lanes)] = pair.astype(jnp.bfloat16)
         back[...] = matmul(staged[...], blocks).astype(jnp.bfloat16)
 
-    def backward_x(c, source, weight, accumulate):
-        potential = matmul(blocks, back[pl.ds(c * wide, wide), :])
-        for q in range(STACK):
-            place = pl.ds(c * chunk + q * wide, wide)
-            part = weight * potential[q * n:(q + 1) * n] * source[:, place].astype(jnp.float32)
-            field[:, place] = field[:, place] + part if accumulate else part
+    def backward_x(group_of_chunks, source, weight, accumulate):
+        operand = jnp.concatenate([back[pl.ds(c * wide, wide), :] for c in group_of_chunks], axis=1)
+        potential = matmul(blocks, operand)
+        for step, c in enumerate(group_of_chunks):
+            for q in range(STACK):
+                place = pl.ds(c * chunk + q * wide, wide)
+                piece = potential[q * n:(q + 1) * n, step * wide:(step + 1) * wide]
+                part = weight * piece * source[:, place].astype(jnp.float32)
+                field[:, place] = field[:, place] + part if accumulate else part
 
     local[2].wait()
     ky_lane = lax.broadcasted_iota(jnp.int32, (n, lanes), 1)
@@ -173,8 +176,7 @@
     middle()
     backward_z()
     weight = occupation(label_own[0:1, :], orbital_count)
-    for c in range(chunks):
-        backward_x(c, own, weight, False)
+    backward_x(range(chunks), own, weight, False)
 
     for c in range(chunks):
         sent[c].wait_recv()
@@ -185,7 +187,8 @@
     weight = occupation(label_other[0:1, :], orbital_count)
     passed = []
     for c in range(chunks):
-        backward_x(c, other, weight, True)
+        if c % 2 == 0:
+            backward_x(range(c, min(c + 2, chunks)), other, weight, True)
         for k, peer in enumerate(peers):
             give[k, :, columns(c)] = field[pl.ds(pl.multiple_of(peer * rows, rows), rows), columns(c)].astype(jnp.bfloat16)
             copy = pltpu.make_async_remote_copy(
@@ -194,18 +197,24 @@
                 device_id={"group": peer}, device_id_type=mesh_id)
             copy.start()
             passed.append((c, k, copy))
+    finished = []
     for c in range(chunks):
         total = field[pl.ds(pl.multiple_of(group * rows, rows), rows), columns(c)]
         for at, k, copy in passed:
             if at == c:
                 copy.wait_recv()
                 total = total + take[k, :, columns(c)].astype(jnp.float32)
-        out_ref[0, :, columns(c)] = -total
+        result_part[:, columns(c)] = -total
+        finished.append(pltpu.make_async_copy(
+            result_part.at[:, columns(c)], out_hbm.at[0, :, columns(c)], out_sem.at[c]))
+        finished[-1].start()
     for _, _, copy in passed:
         copy.wait_send()
     for copy in sent:
         copy.wait_send()
     label_copy.wait_send()
+    for copy in finished:
+        copy.wait()
 
 
 def shards(trial, orbitals, labels, kernel_mask):
@@ -214,16 +223,16 @@
     rows = n // groups
     chunks = n // (STACK * STACK)
     peers = groups - 1
-    vmem = pl.BlockSpec(memory_space=pltpu.VMEM)
     hbm = pl.BlockSpec(memory_space=pltpu.HBM)
     dma = pltpu.SemaphoreType.DMA
     return pl.pallas_call(
         functools.partial(exchange_kernel, n, bands, groups),
         out_shape=jax.ShapeDtypeStruct((1, rows, n * n), jnp.float32),
         in_specs=[hbm, hbm, pl.BlockSpec(memory_space=pltpu.SMEM), hbm, hbm],
-        out_specs=vmem,
+        out_specs=hbm,
         scratch_shapes=[
             pltpu.VMEM((STACK * n, STACK * n), jnp.bfloat16),
+            pltpu.VMEM((rows, n * n), jnp.float32),
             pltpu.VMEM((n, n * n), jnp.bfloat16),
             pltpu.VMEM((n, n * n), jnp.bfloat16),
             pltpu.VMEM((n, n * n), jnp.bfloat16),
@@ -239,6 +248,7 @@
             pltpu.VMEM((peers, rows, n * n), jnp.bfloat16),
             pltpu.VMEM((peers, rows, n * n), jnp.bfloat16),
             dma((4,)), dma((chunks,)), dma((chunks,)), dma, dma, dma((peers, chunks)), dma((peers, chunks)),
+            dma((chunks,)),
         ],
         compiler_params=pltpu.CompilerParams(
             collective_id=0, has_side_effects=True, vmem_limit_bytes=63 * 1024 * 1024),

time: 24.7 us -> 24.6 us (level)
  no operation moved by 1% of the time
where the time goes in v5:
time: 24.6 us; the launch traced here: 24.4 us
  Pallas kernels  21.9 us (89%)
  local copies, waits for them, and re-layouts  1.87 us (8%)
  between operations  0.66 us (3%)
    pallas_call x1, Pallas kernels, shards(): pl.pallas_call(functools.partial(exchange_kernel, n, bands, groups), out_...  21.9 us
    unnamed x1, local copies, waits for them, and re-layouts  1.87 us

profile of v5, /device:TPU:31, one launch (start us, length us, event | category | flops | bytes accessed | tf_op | source)
XLA Modules:
  0.0 24.4 jit_solution(15742964657335787407)
XLA Ops:
  0.7 21.9 %exchange.1 = f32[1,32,4096]{2,1,0:T(8,128)} custom-call(bf16[1,64,4096]{2,1,0:T(8,128)(2,1)} %trial_hbm.1, bf16[1,64,4096]{2,1,0:T(8,128)(2,1)} %orbital_hbm.1, s32[1]{0:T(128)S(6)} %copy.7.label_ref, s32[64,4096]{1,0:T(8,128)} %mask_hbm.1, bf16[256,256]{1,0:T(8,128)(2,1)} %constant.2.clone.blocks_hbm), custom_call_target="tpu_custom_call" | custom-call | tf_op jit(solution)/shard_map/exchange/pallas_call | solution.py:228
  22.5 1.9 %copy.8 = f32[1,32,4096]{2,1,0:T(8,128)} copy(f32[1,32,4096]{2,1,0:T(8,128)} %exchange.1) | data formatting | bytes 1048576

commit v6 on v5

--- a/solution.py
+++ b/solution.py
@@ -251,7 +251,7 @@
             dma((chunks,)),
         ],
         compiler_params=pltpu.CompilerParams(
-            collective_id=0, has_side_effects=True, vmem_limit_bytes=63 * 1024 * 1024),
+            collective_id=0, has_side_effects=True, vmem_limit_bytes=53 * 1024 * 1024),
         name="exchange",
     )(trial, orbitals, labels, kernel_mask, cas_blocks(n))
 

time: 24.6 us -> 24 us (0.976)
  Pallas kernels: 21.9 us -> 21.4 us
    pallas_call x1, Pallas kernels: 21.9 us -> 21.4 us  [shards(): pl.pallas_call(functools.partial(exchange_kernel, n, bands, groups), out_...]
    unnamed x1 -> x3, local copies, waits for them, and re-layouts: 1.87 us -> 1.7 us
where the time goes in v6:
time: 24 us; the launch traced here: 23.8 us
  Pallas kernels  21.4 us (89%)
  local copies, waits for them, and re-layouts  1.7 us (7%)
  between operations  0.67 us (3%)
    pallas_call x1, Pallas kernels, shards(): pl.pallas_call(functools.partial(exchange_kernel, n, bands, groups), out_...  21.4 us
    unnamed x3, local copies, waits for them, and re-layouts  1.7 us

profile of v6, /device:TPU:31, one launch (start us, length us, event | category | flops | bytes accessed | tf_op | source)
XLA Modules:
  0.0 23.8 jit_solution(7009518122069433192)
XLA Ops:
  0.7 0.0 copy-start
  0.7 0.9 %copy-done = bf16[256,256]{1,0:T(8,128)(2,1)S(1)} copy-done((bf16[256,256]{1,0:T(8,128)(2,1)S(1)}, bf16[256,256]{1,0:T(8,128)(2,1)}, u32[]{:S(2)}) %copy-start) | copy-done | bytes 131096
  1.6 21.4 %exchange.1 = f32[1,32,4096]{2,1,0:T(8,128)S(1)} custom-call(bf16[1,64,4096]{2,1,0:T(8,128)(2,1)} %trial_hbm.1, bf16[1,64,4096]{2,1,0:T(8,128)(2,1)} %orbital_hbm.1, s32[1]{0:T(128)S(6)} %copy.7.label_ref, s32[64,4096]{1,0:T(8,128)} %mask_hbm.1, bf16[256,256]{1,0:T(8,128)(2,1)S(1)} %copy-done), custom_call_target="tpu_custom_call" | custom-call | tf_op jit(solution)/shard_map/exchange/pallas_call | solution.py:228
  23.0 0.8 %copy.8 = f32[1,32,4096]{2,1,0:T(8,128)} copy(f32[1,32,4096]{2,1,0:T(8,128)S(1)} %exchange.1) | data formatting | bytes 1048576
Async XLA Ops:
  0.7 0.9 %copy-start = (bf16[256,256]{1,0:T(8,128)(2,1)S(1)}, bf16[256,256]{1,0:T(8,128)(2,1)}, u32[]{:S(2)}) copy-start(bf16[256,256]{1,0:T(8,128)(2,1)} %constant.2.clone.blocks_hbm) | copy-start | bytes 393220

commit v7 on v6

--- a/solution.py
+++ b/solution.py
@@ -77,11 +77,12 @@
             src_ref=orbital_hbm.at[0, :, columns(c)], dst_ref=other.at[:, columns(c)],
             send_sem=send_sem.at[c], recv_sem=recv_sem.at[c],
             device_id={"band": before}, device_id_type=mesh_id))
-        sent[-1].start()
     label_copy = pltpu.make_async_remote_copy(
         src_ref=label_own, dst_ref=label_other, send_sem=label_send, recv_sem=label_recv,
         device_id={"band": before}, device_id_type=mesh_id)
     label_copy.start()
+    for copy in sent[:-1]:
+        copy.start()
 
     left = lax.broadcasted_iota(jnp.int32, (half, lanes), 1) < n
 
@@ -178,6 +179,8 @@
     weight = occupation(label_own[0:1, :], orbital_count)
     backward_x(range(chunks), own, weight, False)
 
+    sent[0].wait_send()
+    sent[-1].start()
     for c in range(chunks):
         sent[c].wait_recv()
         forward([c], other)
@@ -210,7 +213,7 @@
         finished[-1].start()
     for _, _, copy in passed:
         copy.wait_send()
-    for copy in sent:
+    for copy in sent[1:]:
         copy.wait_send()
     label_copy.wait_send()
     for copy in finished:

time: 24 us -> 24 us (level)
  no operation moved by 1% of the time
where the time goes in v7:
time: 24 us; the launch traced here: 23.8 us
  Pallas kernels  21.4 us (89%)
  local copies, waits for them, and re-layouts  1.7 us (7%)
  between operations  0.67 us (3%)
    pallas_call x1, Pallas kernels, shards(): pl.pallas_call(functools.partial(exchange_kernel, n, bands, groups), out_...  21.4 us
    unnamed x3, local copies, waits for them, and re-layouts  1.7 us

profile of v7, /device:TPU:31, one launch (start us, length us, event | category | flops | bytes accessed | tf_op | source)
XLA Modules:
  0.0 23.8 jit_solution(12806643343886016062)
XLA Ops:
  0.7 0.0 copy-start
  0.7 0.9 %copy-done = bf16[256,256]{1,0:T(8,128)(2,1)S(1)} copy-done((bf16[256,256]{1,0:T(8,128)(2,1)S(1)}, bf16[256,256]{1,0:T(8,128)(2,1)}, u32[]{:S(2)}) %copy-start) | copy-done | bytes 131096
  1.6 21.4 %exchange.1 = f32[1,32,4096]{2,1,0:T(8,128)S(1)} custom-call(bf16[1,64,4096]{2,1,0:T(8,128)(2,1)} %trial_hbm.1, bf16[1,64,4096]{2,1,0:T(8,128)(2,1)} %orbital_hbm.1, s32[1]{0:T(128)S(6)} %copy.7.label_ref, s32[64,4096]{1,0:T(8,128)} %mask_hbm.1, bf16[256,256]{1,0:T(8,128)(2,1)S(1)} %copy-done), custom_call_target="tpu_custom_call" | custom-call | tf_op jit(solution)/shard_map/exchange/pallas_call | solution.py:231
  23.0 0.8 %copy.8 = f32[1,32,4096]{2,1,0:T(8,128)} copy(f32[1,32,4096]{2,1,0:T(8,128)S(1)} %exchange.1) | data formatting | bytes 1048576
Async XLA Ops:
  0.7 0.9 %copy-start = (bf16[256,256]{1,0:T(8,128)(2,1)S(1)}, bf16[256,256]{1,0:T(8,128)(2,1)}, u32[]{:S(2)}) copy-start(bf16[256,256]{1,0:T(8,128)(2,1)} %constant.2.clone.blocks_hbm) | copy-start | bytes 393220

commit v8 on v7

--- a/solution.py
+++ b/solution.py
@@ -2,7 +2,6 @@
 
 import jax
 import jax.numpy as jnp
-import ml_dtypes
 import numpy as np
 from jax import lax
 from jax.experimental import pallas as pl
@@ -16,11 +15,15 @@
 
 
 def cas_blocks(grid_size):
-    frequency = np.arange(grid_size)
-    angle = (np.outer(frequency, frequency) % grid_size) * (2.0 * np.pi / grid_size)
-    table = (np.cos(angle) + np.sin(angle)) / np.sqrt(grid_size)
-    blocks = np.kron(np.eye(STACK), table).astype(np.float32)
-    return jnp.asarray(blocks.astype(ml_dtypes.bfloat16))
+    shape = (grid_size, 2 * grid_size)
+    row = lax.broadcasted_iota(jnp.int32, shape, 0)
+    column = lax.rem(lax.broadcasted_iota(jnp.int32, shape, 1), grid_size)
+    angle = lax.rem(row * column, grid_size).astype(jnp.float32) * (2.0 * np.pi / grid_size)
+    table = (jnp.cos(angle) + jnp.sin(angle)) * np.float32(1.0 / np.sqrt(grid_size))
+    table = jnp.concatenate([table] * (STACK // 2), axis=1)
+    owner = lax.broadcasted_iota(jnp.int32, table.shape, 1) // grid_size
+    blocks = [jnp.where(owner == block, table, 0.0) for block in range(STACK)]
+    return jnp.concatenate(blocks, axis=0).astype(jnp.bfloat16)
 
 
 def occupation(label_values, orbital_count):
@@ -35,7 +38,7 @@
 
 def exchange_kernel(
     n, bands, groups,
-    trial_hbm, orbital_hbm, label_ref, mask_hbm, blocks_hbm, out_hbm,
+    trial_hbm, orbital_hbm, label_ref, mask_hbm, out_hbm,
     table, result_part, target, own, other, mask, staged, back, cube, filtered, coulomb, field, label_own, label_other,
     give, take, local_sem, send_sem, recv_sem, label_send, label_recv, give_sem, take_sem, out_sem,
 ):
@@ -57,9 +60,8 @@
         pltpu.make_async_copy(orbital_hbm.at[0], own, local_sem.at[0]),
         pltpu.make_async_copy(trial_hbm.at[0], target, local_sem.at[1]),
         pltpu.make_async_copy(mask_hbm, mask, local_sem.at[2]),
-        pltpu.make_async_copy(blocks_hbm, table, local_sem.at[3]),
     ]
-    for at in (2, 0, 1, 3):
+    for at in (2, 0, 1):
         local[at].start()
     label_own[...] = jnp.full(label_own.shape, label_ref[0], jnp.int32)
 
@@ -159,6 +161,7 @@
                 part = weight * piece * source[:, place].astype(jnp.float32)
                 field[:, place] = field[:, place] + part if accumulate else part
 
+    table[...] = cas_blocks(n)
     local[2].wait()
     ky_lane = lax.broadcasted_iota(jnp.int32, (n, lanes), 1)
     kx_row = lax.broadcasted_iota(jnp.int32, (n, lanes), 0)
@@ -170,7 +173,6 @@
 
     local[0].wait()
     local[1].wait()
-    local[3].wait()
     blocks = table[...]
     orbital_count = bands * groups
     forward(range(chunks), own)
@@ -231,7 +233,7 @@
     return pl.pallas_call(
         functools.partial(exchange_kernel, n, bands, groups),
         out_shape=jax.ShapeDtypeStruct((1, rows, n * n), jnp.float32),
-        in_specs=[hbm, hbm, pl.BlockSpec(memory_space=pltpu.SMEM), hbm, hbm],
+        in_specs=[hbm, hbm, pl.BlockSpec(memory_space=pltpu.SMEM), hbm],
         out_specs=hbm,
         scratch_shapes=[
             pltpu.VMEM((STACK * n, STACK * n), jnp.bfloat16),
@@ -250,13 +252,13 @@
             pltpu.VMEM((8, STACK * n), jnp.int32),
             pltpu.VMEM((peers, rows, n * n), jnp.bfloat16),
             pltpu.VMEM((peers, rows, n * n), jnp.bfloat16),
-            dma((4,)), dma((chunks,)), dma((chunks,)), dma, dma, dma((peers, chunks)), dma((peers, chunks)),
+            dma((3,)), dma((chunks,)), dma((chunks,)), dma, dma, dma((peers, chunks)), dma((peers, chunks)),
             dma((chunks,)),
         ],
         compiler_params=pltpu.CompilerParams(
             collective_id=0, has_side_effects=True, vmem_limit_bytes=53 * 1024 * 1024),
         name="exchange",
-    )(trial, orbitals, labels, kernel_mask, cas_blocks(n))
+    )(trial, orbitals, labels, kernel_mask)
 
 
 def solution(mesh):

time: 24 us -> 22.9 us (0.954)
  local copies, waits for them, and re-layouts: 1.7 us -> 0.8 us
    unnamed x3 -> x1, local copies, waits for them, and re-layouts: 1.7 us -> 0.8 us
where the time goes in v8:
time: 22.9 us; the launch traced here: 22.7 us
  Pallas kernels  21.3 us (93%)
  local copies, waits for them, and re-layouts  0.8 us (3%)
  between operations  0.66 us (3%)
    pallas_call x1, Pallas kernels, shards(): pl.pallas_call(functools.partial(exchange_kernel, n, bands, groups), out_...  21.3 us
    unnamed x1, local copies, waits for them, and re-layouts  0.8 us

profile of v8, /device:TPU:31, one launch (start us, length us, event | category | flops | bytes accessed | tf_op | source)
XLA Modules:
  0.0 22.7 jit_solution(6190343154539748559)
XLA Ops:
  0.7 21.3 %exchange.1 = f32[1,32,4096]{2,1,0:T(8,128)S(1)} custom-call(bf16[1,64,4096]{2,1,0:T(8,128)(2,1)} %trial_hbm.1, bf16[1,64,4096]{2,1,0:T(8,128)(2,1)} %orbital_hbm.1, s32[1]{0:T(128)S(6)} %copy.6.label_ref, s32[64,4096]{1,0:T(8,128)} %mask_hbm.1), custom_call_target="tpu_custom_call" | custom-call | tf_op jit(solution)/shard_map/exchange/pallas_call | solution.py:233
  21.9 0.8 %copy.7 = f32[1,32,4096]{2,1,0:T(8,128)} copy(f32[1,32,4096]{2,1,0:T(8,128)S(1)} %exchange.1) | data formatting | bytes 1048576

commit v9 on v8

--- a/solution.py
+++ b/solution.py
@@ -38,9 +38,9 @@
 
 def exchange_kernel(
     n, bands, groups,
-    trial_hbm, orbital_hbm, label_ref, mask_hbm, out_hbm,
-    table, result_part, target, own, other, mask, staged, back, cube, filtered, coulomb, field, label_own, label_other,
-    give, take, local_sem, send_sem, recv_sem, label_send, label_recv, give_sem, take_sem, out_sem,
+    trial_hbm, orbital_hbm, label_ref, mask_hbm, out_ref,
+    table, target, own, other, mask, staged, back, cube, filtered, coulomb, field, label_own, label_other,
+    give, take, local_sem, send_sem, recv_sem, label_send, label_recv, give_sem, take_sem,
 ):
     band, group = lax.axis_index("band"), lax.axis_index("group")
     before = lax.rem(band + bands - 1, bands)
@@ -56,6 +56,12 @@
     def columns(c):
         return pl.ds(c * chunk, chunk)
 
+    barrier = pltpu.get_barrier_semaphore()
+    peers = [lax.rem(group + k, groups) for k in range(1, groups)]
+    for neighbour in (before, after):
+        pl.semaphore_signal(barrier, inc=1, device_id={"band": neighbour}, device_id_type=mesh_id)
+    for peer in peers:
+        pl.semaphore_signal(barrier, inc=1, device_id={"group": peer}, device_id_type=mesh_id)
     local = [
         pltpu.make_async_copy(orbital_hbm.at[0], own, local_sem.at[0]),
         pltpu.make_async_copy(trial_hbm.at[0], target, local_sem.at[1]),
@@ -65,12 +71,6 @@
         local[at].start()
     label_own[...] = jnp.full(label_own.shape, label_ref[0], jnp.int32)
 
-    barrier = pltpu.get_barrier_semaphore()
-    peers = [lax.rem(group + k, groups) for k in range(1, groups)]
-    for neighbour in (before, after):
-        pl.semaphore_signal(barrier, inc=1, device_id={"band": neighbour}, device_id_type=mesh_id)
-    for peer in peers:
-        pl.semaphore_signal(barrier, inc=1, device_id={"group": peer}, device_id_type=mesh_id)
     pl.semaphore_wait(barrier, 2 + len(peers))
 
     sent = []
@@ -202,24 +202,18 @@
                 device_id={"group": peer}, device_id_type=mesh_id)
             copy.start()
             passed.append((c, k, copy))
-    finished = []
     for c in range(chunks):
         total = field[pl.ds(pl.multiple_of(group * rows, rows), rows), columns(c)]
         for at, k, copy in passed:
             if at == c:
                 copy.wait_recv()
                 total = total + take[k, :, columns(c)].astype(jnp.float32)
-        result_part[:, columns(c)] = -total
-        finished.append(pltpu.make_async_copy(
-            result_part.at[:, columns(c)], out_hbm.at[0, :, columns(c)], out_sem.at[c]))
-        finished[-1].start()
+        out_ref[0, :, columns(c)] = -total
     for _, _, copy in passed:
         copy.wait_send()
     for copy in sent[1:]:
         copy.wait_send()
     label_copy.wait_send()
-    for copy in finished:
-        copy.wait()
 
 
 def shards(trial, orbitals, labels, kernel_mask):
@@ -234,26 +228,24 @@
         functools.partial(exchange_kernel, n, bands, groups),
         out_shape=jax.ShapeDtypeStruct((1, rows, n * n), jnp.float32),
         in_specs=[hbm, hbm, pl.BlockSpec(memory_space=pltpu.SMEM), hbm],
-        out_specs=hbm,
+        out_specs=pl.BlockSpec(memory_space=pltpu.VMEM),
         scratch_shapes=[
             pltpu.VMEM((STACK * n, STACK * n), jnp.bfloat16),
-            pltpu.VMEM((rows, n * n), jnp.float32),
             pltpu.VMEM((n, n * n), jnp.bfloat16),
             pltpu.VMEM((n, n * n), jnp.bfloat16),
             pltpu.VMEM((n, n * n), jnp.bfloat16),
             pltpu.VMEM((n, n * n), jnp.int32),
             pltpu.VMEM((n * n // STACK, STACK * n), jnp.bfloat16),
             pltpu.VMEM((n * n // STACK, STACK * n), jnp.bfloat16),
-            pltpu.VMEM((n // 2 * (n + PAD), 2 * n), jnp.float32),
-            pltpu.VMEM((n // 2 * (n + PAD), 2 * n), jnp.float32),
-            pltpu.VMEM((n // 2 * (n + PAD), 2 * n), jnp.float32),
+            pltpu.VMEM((n // 2 * (n + PAD) + n, 2 * n), jnp.float32),
+            pltpu.VMEM((n // 2 * (n + PAD) + n, 2 * n), jnp.float32),
+            pltpu.VMEM((n // 2 * (n + PAD) + n, 2 * n), jnp.float32),
             pltpu.VMEM((n, n * n), jnp.float32),
             pltpu.VMEM((8, STACK * n), jnp.int32),
             pltpu.VMEM((8, STACK * n), jnp.int32),
             pltpu.VMEM((peers, rows, n * n), jnp.bfloat16),
             pltpu.VMEM((peers, rows, n * n), jnp.bfloat16),
             dma((3,)), dma((chunks,)), dma((chunks,)), dma, dma, dma((peers, chunks)), dma((peers, chunks)),
-            dma((chunks,)),
         ],
         compiler_params=pltpu.CompilerParams(
             collective_id=0, has_side_effects=True, vmem_limit_bytes=53 * 1024 * 1024),

time: 22.9 us -> 22.8 us (level)
  no operation moved by 1% of the time
where the time goes in v9:
time: 22.8 us; the launch traced here: 22.6 us
  Pallas kernels  21.2 us (93%)
  local copies, waits for them, and re-layouts  0.8 us (4%)
  between operations  0.66 us (3%)
    pallas_call x1, Pallas kernels, shards(): pl.pallas_call(functools.partial(exchange_kernel, n, bands, groups), out_...  21.2 us
    unnamed x1, local copies, waits for them, and re-layouts  0.8 us

profile of v9, /device:TPU:31, one launch (start us, length us, event | category | flops | bytes accessed | tf_op | source)
XLA Modules:
  0.0 22.6 jit_solution(15017754579325983107)
XLA Ops:
  0.7 21.2 %exchange.1 = f32[1,32,4096]{2,1,0:T(8,128)S(1)} custom-call(bf16[1,64,4096]{2,1,0:T(8,128)(2,1)} %trial_hbm.1, bf16[1,64,4096]{2,1,0:T(8,128)(2,1)} %orbital_hbm.1, s32[1]{0:T(128)S(6)} %copy.6.label_ref, s32[64,4096]{1,0:T(8,128)} %mask_hbm.1), custom_call_target="tpu_custom_call" | custom-call | tf_op jit(solution)/shard_map/exchange/pallas_call | solution.py:227
  21.8 0.8 %copy.7 = f32[1,32,4096]{2,1,0:T(8,128)} copy(f32[1,32,4096]{2,1,0:T(8,128)S(1)} %exchange.1) | data formatting | bytes 1048576
